TPU v7x, 128 devices: a whole 4x4x4 slice. The times are simulated.
128 devices in a mesh: row: 8 (over y, z_lo), col: 16 (over x, z_hi, core).
Axes of the slice: x: 4, y: 4, z: 4 (z_hi: 2, z_lo: 2; z = z_hi * 2 + z_lo), core: 2. Of those that a mesh axis runs over, the one named last changes fastest.
Arguments:
- factor: float32 [10240, 8192], P('row', 'col'), may hold values from -0.09375 to 0.09375
- inverse: float32 [2, 4096, 4096], P(None, 'row', 'col'), may hold values from -0.09375 to 0.09375
- rhs: float32 [10240, 1024], P('row'), may hold values from -6 to 6
Outputs:
- solved: float32 [10240, 1024], P('row')
All inputs are finite; a program needn't handle non-finite values.
Results may differ from a plain program's by a relative error of at most 0.000078.
Values sent between devices are 32-bit elements; how exact they have to be, the bound alone decides.
A program may use at most 64 MiB of HBM per device.

v0:
```python
import jax
import jax.numpy as jnp
from jax import lax
from jax.sharding import PartitionSpec as P


def broadcast(value, axis, root):
    mine = lax.axis_index(axis) == root
    return lax.psum(jnp.where(mine, value, jnp.zeros_like(value)), axis)


def matmul(left, right):
    return jnp.dot(left, right, precision=lax.Precision.HIGHEST, preferred_element_type=jnp.float32)


def shards(factor, inverse, rhs):
    row_count = lax.axis_size("row")
    tile = inverse.shape[2]
    panel_tiles = inverse.shape[1] // tile
    held_tiles = rhs.shape[0] // tile
    first_panel = held_tiles - 2 * panel_tiles
    column_id = lax.axis_index("col")
    source_row = column_id % row_count
    local_slot = column_id // row_count * tile
    current = rhs
    for panel in (1, 0):
        solve_current = current
        begin = (first_panel + panel * panel_tiles) * tile
        finish = begin + panel_tiles * tile
        own_rows = solve_current[begin:finish]
        piece = lax.dynamic_slice_in_dim(own_rows, local_slot, tile, 0)
        piece = broadcast(piece, "row", source_row)
        partial_value = matmul(inverse[panel], piece)
        solution = lax.psum(partial_value, "col")
        solve_current = jnp.concatenate(
            [solve_current[:begin], solution, solve_current[finish:]], axis=0
        )
        solve_solution_tile = lax.dynamic_slice_in_dim(solution, local_slot, tile, 0)
        solve_solution_tile = broadcast(solve_solution_tile, "row", source_row)
        current = solve_current
        limit = first_panel + panel * panel_tiles
        block = factor[0 * tile : limit * tile, panel * tile : (panel + 1) * tile]
        total = lax.psum(matmul(block, solve_solution_tile), "col")
        current = jnp.concatenate(
            [current[: limit * tile] - total, current[limit * tile :]], axis=0
        )
    return current


def solution(mesh):
    return jax.shard_map(
        shards,
        mesh=mesh,
        in_specs=(P("row", "col"), P(None, "row", "col"), P("row", None)),
        out_specs=P("row", None),
        check_vma=False,
    )
```

profile of v0, /device:TPU:1, one launch (start us, length us, event | category | flops | bytes accessed | tf_op | source)
XLA Modules:
  0.0 949.8 jit_solution(13570268178226142160)
XLA Ops:
  6.5 0.0 slice-start
  6.5 0.0 all-reduce.9.cloned.1.call-start
  6.5 1.6 slice-done
  8.1 0.1 constant_dynamic-slice_fusion
  8.2 0.0 copy-start.1
  8.2 0.3 copy.9
  8.6 1.0 broadcast_select_fusion
  9.6 0.0 all-reduce.9.cloned.1.call-update
  9.7 0.0 all-reduce.11.cloned.1.call-start
  9.7 77.1 %all-reduce.9.cloned.1.call-done = f32[256,1024]{0,1:T(8,128)} async-done(((f32[256,1024]{0,1:T(8,128)}), f32[256,1024]{0,1:T(8,128)}) %all-reduce.9.cloned.1.call-update) | async-done | bytes 1048592 | tf_op jit(solution)/shard_map/psum | solution.py:9
  86.8 0.0 copy-done.1
  86.8 4.4 convolution_bitcast_fusion.2
  91.2 0.0 all-reduce.11.cloned.1.call-update
  91.2 0.0 all-reduce.13.cloned.1.call-start
  91.3 147.9 %all-reduce.11.cloned.1.call-done = f32[512,1024]{0,1:T(8,128)} async-done(((f32[512,1024]{0,1:T(8,128)}), f32[512,1024]{0,1:T(8,128)}) %all-reduce.11.cloned.1.call-update) | async-done | bytes 2097168 | tf_op jit(solution)/shard_map/psum | solution.py:34
  239.1 2.3 dynamic-slice_select_fusion.2
  241.4 0.0 all-reduce.13.cloned.1.call-update
  241.4 0.0 all-reduce.15.cloned.1.call-start
  241.5 75.3 %all-reduce.13.cloned.1.call-done = f32[256,1024]{0,1:T(8,128)} async-done(((f32[256,1024]{0,1:T(8,128)}), f32[256,1024]{0,1:T(8,128)}) %all-reduce.13.cloned.1.call-update) | async-done | bytes 1048592 | tf_op jit(solution)/shard_map/psum | solution.py:9
  316.7 5.8 convolution_bitcast_fusion
  322.6 0.0 all-reduce.15.cloned.1.call-update
  322.6 0.0 slice-start.1
  322.6 0.0 all-reduce.17.cloned.1.call-start
  322.6 1.8 slice-done.1
  324.5 2.4 copy.7
  326.8 146.9 %all-reduce.15.cloned.1.call-done = f32[768,1024]{0,1:T(8,128)} async-done(((f32[768,1024]{0,1:T(8,128)}), f32[768,1024]{0,1:T(8,128)}) %all-reduce.15.cloned.1.call-update) | async-done | bytes 3145744 | tf_op jit(solution)/shard_map/psum | solution.py:43
  473.8 3.2 sub.11
  477.0 0.2 slice.33
  477.3 1.1 dynamic-slice_select_fusion.1
  478.4 0.0 all-reduce.17.cloned.1.call-update
  478.4 0.0 all-reduce.19.cloned.1.call-start
  478.4 75.0 %all-reduce.17.cloned.1.call-done = f32[256,1024]{0,1:T(8,128)} async-done(((f32[256,1024]{0,1:T(8,128)}), f32[256,1024]{0,1:T(8,128)}) %all-reduce.17.cloned.1.call-update) | async-done | bytes 1048592 | tf_op jit(solution)/shard_map/psum | solution.py:9
  553.4 4.5 convolution_bitcast_fusion.1
  557.9 0.0 all-reduce.19.cloned.1.call-update
  558.0 0.0 all-reduce.21.cloned.1.call-start
  558.0 147.9 %all-reduce.19.cloned.1.call-done = f32[512,1024]{0,1:T(8,128)} async-done(((f32[512,1024]{0,1:T(8,128)}), f32[512,1024]{0,1:T(8,128)}) %all-reduce.19.cloned.1.call-update) | async-done | bytes 2097168 | tf_op jit(solution)/shard_map/psum | solution.py:34
  705.9 2.3 dynamic-slice_select_fusion
  708.2 0.0 all-reduce.21.cloned.1.call-update
  708.2 0.0 all-reduce.23.cloned.1.call-start
  708.2 75.1 %all-reduce.21.cloned.1.call-done = f32[256,1024]{0,1:T(8,128)} async-done(((f32[256,1024]{0,1:T(8,128)}), f32[256,1024]{0,1:T(8,128)}) %all-reduce.21.cloned.1.call-update) | async-done | bytes 1048592 | tf_op jit(solution)/shard_map/psum | solution.py:9
  783.4 3.3 convolution_bitcast_fusion.3
  786.6 0.0 all-reduce.23.cloned.1.call-update
  786.6 144.2 %all-reduce.23.cloned.1.call-done = f32[256,1024]{0,1:T(8,128)} async-done(((f32[256,1024]{0,1:T(8,128)}), f32[256,1024]{0,1:T(8,128)}) %all-reduce.23.cloned.1.call-update) | async-done | bytes 1048592 | tf_op jit(solution)/shard_map/psum | solution.py:43
  930.9 0.0 copy-start
  930.9 1.5 slice_subtract_fusion
  932.4 0.4 copy-done
  932.8 4.3 pad_maximum_fusion
  937.1 5.9 copy.6
Async XLA Ops:
  6.5 1.6 slice-start
  6.5 80.3 %all-reduce.9.cloned.1.call-start = ((), (), s32[]{:S(2)}) async-start(), calls=%async_computation | async-start | bytes 2097152 | tf_op jit(solution)/shard_map/psum | solution.py:9
  8.2 78.6 %copy-start.1 = (f32[2,512,256]{2,1,0:T(8,128)S(1)}, f32[2,512,256]{2,1,0:T(8,128)}, u32[]{:S(2)}) copy-start(f32[2,512,256]{2,1,0:T(8,128)} %param.4) | copy-start | bytes 3145732
  9.7 229.5 %all-reduce.11.cloned.1.call-start = ((), (), s32[]{:S(2)}) async-start(), calls=%async_computation.1 | async-start | bytes 4194304 | tf_op jit(solution)/shard_map/psum | solution.py:34
  91.2 225.5 %all-reduce.13.cloned.1.call-start = ((), (), s32[]{:S(2)}) async-start(), calls=%async_computation.2 | async-start | bytes 2097152 | tf_op jit(solution)/shard_map/psum | solution.py:9
  241.4 232.4 %all-reduce.15.cloned.1.call-start = ((), (), s32[]{:S(2)}) async-start(), calls=%async_computation.3 | async-start | bytes 6291456 | tf_op jit(solution)/shard_map/psum | solution.py:43
  322.6 1.9 slice-start.1
  322.6 230.8 %all-reduce.17.cloned.1.call-start = ((), (), s32[]{:S(2)}) async-start(), calls=%async_computation.4 | async-start | bytes 2097152 | tf_op jit(solution)/shard_map/psum | solution.py:9
  478.4 227.5 %all-reduce.19.cloned.1.call-start = ((), (), s32[]{:S(2)}) async-start(), calls=%async_computation.5 | async-start | bytes 4194304 | tf_op jit(solution)/shard_map/psum | solution.py:34
  558.0 225.4 %all-reduce.21.cloned.1.call-start = ((), (), s32[]{:S(2)}) async-start(), calls=%async_computation.6 | async-start | bytes 2097152 | tf_op jit(solution)/shard_map/psum | solution.py:9
  708.2 222.7 %all-reduce.23.cloned.1.call-start = ((), (), s32[]{:S(2)}) async-start(), calls=%async_computation.7 | async-start | bytes 2097152 | tf_op jit(solution)/shard_map/psum | solution.py:43
  930.9 1.9 copy-start
Sparse Core Ops, SparseCore 0:
  9.9 76.9 all-reduce.8
  91.3 147.7 all-reduce.10
  241.6 75.0 all-reduce.12
  322.7 151.0 all-reduce.14
  478.5 74.8 all-reduce.16
  558.1 147.7 all-reduce.18
  708.4 74.9 all-reduce.20
  786.8 144.0 all-reduce.22
where the time goes:
time: 950 us
  waiting for transfers between devices  890 us (94%)
  matrix products  18 us (2%)
  other arithmetic  15.7 us (2%)
  between operations  13.6 us (1%)
  local copies, waits for them, and re-layouts  12.7 us (1%)
    psum x4, waiting for transfers between devices, broadcast(): return lax.psum(jnp.where(mine, value, jnp.zeros_like(value)), axis)  302 us
    psum x2, waiting for transfers between devices, shards(): solution = lax.psum(partial_value, 'col')  296 us
    psum x2, waiting for transfers between devices, shards(): total = lax.psum(matmul(block, solve_solution_tile), 'col')  291 us
  transfers between devices with their start and end apart: 8, of which 8 were waited for; matrix products, arithmetic and copies ran while one was open for 0% of the time, Pallas kernels for 0%

commit v1 on v0

v1 whole, which is shorter than its diff:
```python
import functools

import jax
import jax.numpy as jnp
from jax import lax
from jax.experimental import pallas as pl
from jax.experimental.pallas import tpu as pltpu
from jax.sharding import PartitionSpec as P

MESH = pl.DeviceIdType.MESH
T = 256
W = 128
NY = 4
NQ = 8
NCH = 8


def kernel(fac, inv, rhs, out,
           G, PT, RB, XB, XS, B0, PA, RA, AT, AB, RH, OA,
           lsem, bsem, bss, gss, grs, dss, drs, rss, rrs, ass, ars,
           zss, zrs, oss, ors, fss, frs):
    row = lax.axis_index("row")
    col = lax.axis_index("col")
    y, zl = lax.div(row, 2), lax.rem(row, 2)
    Q, c = lax.div(col, 2), lax.rem(col, 2)
    yo, so = lax.rem(Q, NY), lax.div(Q, NY)

    def dev(y_, zl_, q_, c_):
        return (2 * y_ + zl_, 2 * q_ + c_)

    def yy(d):
        return lax.rem(y + d, NY)

    up, down, far = yy(1), yy(3), yy(2)
    home = y == yo

    def remote(src, dst, ssem, rsem, device):
        return pltpu.make_async_remote_copy(
            src_ref=src, dst_ref=dst, send_sem=ssem, recv_sem=rsem,
            device_id=device, device_id_type=MESH)

    def signal(device):
        pl.semaphore_signal(bar, inc=1, device_id=device, device_id_type=MESH)

    bar = pltpu.get_barrier_semaphore()
    for d in (1, 2, 3):
        signal(dev(yy(d), zl, Q, c))
    signal(dev(y, zl, Q, 1 - c))
    signal(dev(y, 1 - zl, Q, c))
    for d in range(1, NQ):
        signal(dev(y, zl, lax.rem(Q + d, NQ), c))
    for s in range(2):
        for d in range(NY):
            yd = yy(d)
            if d == 0:
                @pl.when(Q != y + NY * s)
                def _():
                    signal(dev(y, zl, y + NY * s, c))
            else:
                signal(dev(yd, zl, y + NY * s, c))
    pl.semaphore_wait(bar, 12 + 8 - jnp.where(home, 1, 0).astype(jnp.int32))

    def own(i):
        if i < 2:
            return inv.at[1, pl.ds(T * i, T), :]
        if i < 4:
            return fac.at[pl.ds(T * (i - 1), T), pl.ds(T, T)]
        if i < 6:
            return inv.at[0, pl.ds(T * (i - 4), T), :]
        if i == 6:
            return fac.at[pl.ds(0, T), pl.ds(T, T)]
        return fac.at[pl.ds(0, T), pl.ds(0, T)]

    def blk(i, yb):
        return G.at[i, c, yb]

    def own_up(i):
        return remote(own(i), blk(i, y), gss.at[i, 0], grs.at[i, 0], dev(up, zl, Q, c))

    def own_down(i):
        return remote(own(i), blk(i, y), gss.at[i, 1], grs.at[i, 1], dev(down, zl, Q, c))

    def relay_up(i):
        r = G.at[i, c, down, pl.ds(0, T // 2), :]
        return remote(r, r, gss.at[i, 2], grs.at[i, 2], dev(up, zl, Q, c))

    def relay_down(i):
        r = G.at[i, c, up, pl.ds(T // 2, T // 2), :]
        return remote(r, r, gss.at[i, 3], grs.at[i, 3], dev(down, zl, Q, c))

    sib = dev(y, zl, Q, 1 - c)

    def share(i, j):
        yb = (y, down, up, far)[j]
        src = own(i) if j == 0 else blk(i, yb)
        return remote(src, blk(i, yb), dss.at[i, j], drs.at[i, j], sib)

    def wait_block(i, yb, sem):
        r = blk(i, yb)
        pltpu.make_async_copy(r, r, sem).wait()

    def wait_half(i, half, sem):
        r = G.at[i, c, far, pl.ds(half * (T // 2), T // 2), :]
        pltpu.make_async_copy(r, r, sem).wait()

    def wait_share(i, j):
        yb = (y, down, up, far)[j]
        r = G.at[i, 1 - c, yb]
        pltpu.make_async_copy(r, r, drs.at[i, j]).wait()

    def send_own(i):
        own_up(i).start()
        own_down(i).start()

    def near(i):
        wait_block(i, down, grs.at[i, 0])
        relay_up(i).start()
        wait_block(i, up, grs.at[i, 1])
        relay_down(i).start()
        share(i, 1).start()
        share(i, 2).start()
        if i + 2 < NCH:
            send_own(i + 2)

    def distant(i):
        wait_half(i, 0, grs.at[i, 2])
        wait_half(i, 1, grs.at[i, 3])
        share(i, 3).start()

    def cols(y_, c_):
        return pl.ds(pl.multiple_of((c_ * NY + y_) * W, W), W)

    def rows(b):
        return pl.ds(pl.multiple_of(b * T, T), T)

    def b_dst(n):
        return XB.at[0, zl] if n == 0 else B0

    def b_move(n, d):
        b = (3 if n == 0 else 1) + so
        yd = yy(d)
        return remote(rhs.at[rows(b), cols(yd, c)], b_dst(n),
                      bss.at[n, d], bsem.at[n], dev(yd, zl, Q, c))

    def b_local(n):
        b = (3 if n == 0 else 1) + so
        return pltpu.make_async_copy(rhs.at[rows(b), cols(y, c)], b_dst(n), bsem.at[n])

    def zmove(st):
        return remote(XB.at[st, zl], XB.at[st, zl], zss.at[st], zrs.at[st],
                      dev(y, 1 - zl, Q, c))

    def zwait(st):
        r = XB.at[st, 1 - zl]
        pltpu.make_async_copy(r, r, zrs.at[st]).wait()

    def split(st, k):
        v = XB[st, k]
        hi = v.astype(jnp.bfloat16)
        lo = (v - hi.astype(jnp.float32)).astype(jnp.bfloat16)
        XS[st, k, :, pl.ds(0, W)] = hi
        XS[st, k, :, pl.ds(W, W)] = lo

    def product(i, yb, st):
        total = None
        for k in range(2):
            a = G[i, k, yb]
            hi = a.astype(jnp.bfloat16)
            lo = (a - hi.astype(jnp.float32)).astype(jnp.bfloat16)
            x = XS[st, k]
            wide = jnp.dot(hi, x, preferred_element_type=jnp.float32)
            part = wide[:, :W] + wide[:, W:] + jnp.dot(
                lo, x[:, :W], preferred_element_type=jnp.float32)
            total = part if total is None else total + part
        return total

    def scatter(ph, t):
        return remote(PT.at[ph, t], RB.at[ph, Q], rss.at[ph, t], rrs.at[ph, Q],
                      dev(y, zl, t, c))

    def tiles(i, ph, st, lo, hi):
        s = i % 2

        def step(j, carry):
            yb = lax.rem(y + 3 + j, NY)
            t = NY * s + yb
            PT[ph, t] = product(i, yb, st)

            @pl.when(t != Q)
            def _():
                scatter(ph, t).start()
            return carry

        lax.fori_loop(lo, hi, step, 0)

    def gathered(ph):
        def step(d, total):
            src = lax.rem(Q + d, NQ)
            r = RB.at[ph, src]
            pltpu.make_async_copy(r, r, rrs.at[ph, src]).wait()
            return total + RB[ph, src]
        return lax.fori_loop(1, NQ, step, PT[ph, Q])

    def o_send(n, d):
        qd = lax.rem(Q + d, NQ)
        st = 1 if n == 1 else 3
        src = XB.at[st, zl]
        dst = out.at[rows(1 + 2 * n + so), cols(y, c)]
        return src, dst, qd

    def o_start(n):
        for d in range(NQ):
            src, dst, qd = o_send(n, d)
            if d == 0:
                @pl.when(home)
                def _():
                    pltpu.make_async_copy(src, dst, ors.at[n, NY * so + y]).start()

                @pl.when(jnp.logical_not(home))
                def _():
                    remote(src, dst, oss.at[n, 0], ors.at[n, NY * so + y],
                           dev(yo, zl, Q, c)).start()
            else:
                remote(src, dst, oss.at[n, d], ors.at[n, NY * so + y],
                       dev(yo, zl, qd, c)).start()

    def o_forward(n):
        for s in range(2):
            for yb in range(NY):
                r = out.at[rows(1 + 2 * n + s), cols(yb, c)]
                pltpu.make_async_copy(r, r, ors.at[n, NY * s + yb]).wait()
        o_share(n).start()

    def halfcols(c_):
        return pl.ds(pl.multiple_of(c_ * NY * W, NY * W), NY * W)

    def o_share(n):
        r = out.at[pl.ds((1 + 2 * n) * T, 2 * T), halfcols(c)]
        return remote(r, r, fss.at[n], frs.at[n], sib)

    def o_shared(n):
        r = out.at[pl.ds((1 + 2 * n) * T, 2 * T), halfcols(1 - c)]
        pltpu.make_async_copy(r, r, frs.at[n]).wait()

    for n in range(2):
        @pl.when(home)
        def _():
            b_local(n).start()
            for d in (1, 2, 3):
                b_move(n, d).start()
        if n == 0:
            send_own(0)
            share(0, 0).start()
    locals_ = [pltpu.make_async_copy(own(i), blk(i, y), lsem.at[i]) for i in range(NCH)]
    rh_copy = pltpu.make_async_copy(rhs.at[pl.ds(0, T), :], RH, lsem.at[NCH])
    for cp in locals_:
        cp.start()
    send_own(1)
    for i in range(1, NCH):
        share(i, 0).start()
    rh_copy.start()

    r = b_dst(0)
    pltpu.make_async_copy(r, r, bsem.at[0]).wait()
    zmove(0).start()
    split(0, zl)
    for cp in locals_:
        cp.wait()
    rh_copy.wait()
    near(0)
    zwait(0)
    split(0, 1 - zl)
    wait_share(0, 0)
    wait_share(0, 1)
    wait_share(0, 2)
    tiles(0, 0, 0, 0, 3)
    distant(0)
    wait_share(0, 3)
    tiles(0, 0, 0, 3, 4)

    def second(i, ph, st):
        near(i)
        for j in range(3):
            wait_share(i, j)
        tiles(i, ph, st, 0, 3)
        distant(i)
        wait_share(i, 3)
        tiles(i, ph, st, 3, 4)

    def first(i, ph, st):
        distant(i)
        for j in range(4):
            wait_share(i, j)
        tiles(i, ph, st, 0, 4)

    def finish(ph, st, nxt):
        total = gathered(ph)
        if st == 2:
            pltpu.make_async_copy(B0, B0, bsem.at[1]).wait()
            XB[st, zl] = B0[...] - total
        else:
            XB[st, zl] = total
        zmove(st).start()
        split(st, zl)
        near(nxt)
        if st == 1:
            o_start(1)
        if st == 3:
            o_start(0)
        zwait(st)
        split(st, 1 - zl)

    second(1, 0, 0)
    finish(0, 1, 2)
    first(2, 1, 1)
    second(3, 1, 1)
    finish(1, 2, 4)
    o_forward(1)
    first(4, 2, 2)
    second(5, 2, 2)
    finish(2, 3, 6)

    def a_move(yb, h):
        return remote(PA.at[yb, pl.ds(h * (T // 2), T // 2), :], RA.at[Q],
                      ass.at[NY * h + yb], ars.at[Q], dev(y, zl, NY * h + yb, c))

    def above(lo, hi):
        def step(j, carry):
            yb = lax.rem(y + 3 + j, NY)
            PA[yb] = product(6, yb, 1) + product(7, yb, 3)
            for h in range(2):
                @pl.when(NY * h + yb != Q)
                def _():
                    a_move(yb, h).start()
            return carry
        lax.fori_loop(lo, hi, step, 0)

    distant(6)
    for j in range(4):
        wait_share(6, j)
    near(7)
    for j in range(3):
        wait_share(7, j)
    above(0, 3)
    distant(7)
    wait_share(7, 3)
    above(3, 4)
    o_forward(0)

    def a_step(d, total):
        src = lax.rem(Q + d, NQ)
        r = RA.at[src]
        pltpu.make_async_copy(r, r, ars.at[src]).wait()
        return total + RA[src]

    half = pl.ds(pl.multiple_of(so * (T // 2), T // 2), T // 2)
    AT[...] = lax.fori_loop(1, NQ, a_step, PA[yo, half, :])

    a_dst = AB.at[half, cols(y, c)]
    a_sem = ors.at[2, NY * so + y]

    @pl.when(home)
    def _():
        pltpu.make_async_copy(AT, a_dst, a_sem).start()

    @pl.when(jnp.logical_not(home))
    def _():
        remote(AT, a_dst, oss.at[2, 0], a_sem, dev(yo, zl, Q, c)).start()

    for d in range(1, NQ):
        remote(AT, a_dst, oss.at[2, d], a_sem,
               dev(yo, zl, lax.rem(Q + d, NQ), c)).start()
    for s in range(2):
        for yb in range(NY):
            r = AB.at[pl.ds(s * (T // 2), T // 2), cols(yb, c)]
            pltpu.make_async_copy(r, r, ors.at[2, NY * s + yb]).wait()
    mine = AB.at[:, halfcols(c)]
    a_share = remote(mine, mine, fss.at[2], frs.at[2], sib)
    a_share.start()
    OA[:, halfcols(c)] = RH[:, halfcols(c)] - AB[:, halfcols(c)]
    w0 = pltpu.make_async_copy(OA.at[:, halfcols(c)], out.at[pl.ds(0, T), halfcols(c)], lsem.at[0])
    w0.start()
    theirs = AB.at[:, halfcols(1 - c)]
    pltpu.make_async_copy(theirs, theirs, frs.at[2]).wait()
    OA[:, halfcols(1 - c)] = RH[:, halfcols(1 - c)] - AB[:, halfcols(1 - c)]
    w1 = pltpu.make_async_copy(OA.at[:, halfcols(1 - c)], out.at[pl.ds(0, T), halfcols(1 - c)], lsem.at[1])
    w1.start()

    o_shared(1)
    o_shared(0)
    w0.wait()
    w1.wait()
    for n in range(2):
        @pl.when(home)
        def _():
            for d in (1, 2, 3):
                b_move(n, d).wait_send()
    for i in range(NCH):
        own_up(i).wait_send()
        own_down(i).wait_send()
        relay_up(i).wait_send()
        relay_down(i).wait_send()
        for j in range(4):
            share(i, j).wait_send()
    for ph in range(3):
        def drain(d, carry):
            scatter(ph, lax.rem(Q + d, NQ)).wait_send()
            return carry
        lax.fori_loop(1, NQ, drain, 0)
    for yb in range(NY):
        for h in range(2):
            @pl.when(NY * h + yb != Q)
            def _():
                a_move(yb, h).wait_send()
    for st in range(4):
        zmove(st).wait_send()
    for n in range(2):
        src, dst, _ = o_send(n, 0)

        @pl.when(jnp.logical_not(home))
        def _():
            remote(src, dst, oss.at[n, 0], ors.at[n, 0], dev(yo, zl, Q, c)).wait_send()
        for d in range(1, NQ):
            src, dst, qd = o_send(n, d)
            remote(src, dst, oss.at[n, d], ors.at[n, 0], dev(yo, zl, qd, c)).wait_send()
        o_share(n).wait_send()

    @pl.when(jnp.logical_not(home))
    def _():
        remote(AT, a_dst, oss.at[2, 0], a_sem, dev(yo, zl, Q, c)).wait_send()
    for d in range(1, NQ):
        remote(AT, a_dst, oss.at[2, d], a_sem,
               dev(yo, zl, lax.rem(Q + d, NQ), c)).wait_send()
    a_share.wait_send()


def shards(factor, inverse, rhs):
    f32, bf16 = jnp.float32, jnp.bfloat16
    dma = pltpu.SemaphoreType.DMA
    return pl.pallas_call(
        kernel,
        out_shape=jax.ShapeDtypeStruct(rhs.shape, f32),
        in_specs=[pl.BlockSpec(memory_space=pl.ANY)] * 3,
        out_specs=pl.BlockSpec(memory_space=pl.ANY),
        scratch_shapes=[
            pltpu.VMEM((NCH, 2, NY, T, T), f32),
            pltpu.VMEM((3, NQ, T, W), f32),
            pltpu.VMEM((3, NQ, T, W), f32),
            pltpu.VMEM((4, 2, T, W), f32),
            pltpu.VMEM((4, 2, T, 2 * W), bf16),
            pltpu.VMEM((T, W), f32),
            pltpu.VMEM((NY, T, W), f32),
            pltpu.VMEM((NQ, T // 2, W), f32),
            pltpu.VMEM((T // 2, W), f32),
            pltpu.VMEM((T, NQ * W), f32),
            pltpu.VMEM((T, NQ * W), f32),
            pltpu.VMEM((T, NQ * W), f32),
            dma((NCH + 1,)),
            dma((2,)), dma((2, 4)),
            dma((NCH, 4)), dma((NCH, 4)),
            dma((NCH, 4)), dma((NCH, 4)),
            dma((3, NQ)), dma((3, NQ)),
            dma((NQ,)), dma((NQ,)),
            dma((4,)), dma((4,)),
            dma((3, NQ)), dma((3, NQ)),
            dma((3,)), dma((3,)),
        ],
        compiler_params=pltpu.CompilerParams(
            collective_id=0, has_side_effects=True, vmem_limit_bytes=56 * 2**20),
        name="panel_steps",
    )(factor, inverse, rhs)


def solution(mesh):
    return jax.shard_map(
        shards,
        mesh=mesh,
        in_specs=(P("row", "col"), P(None, "row", "col"), P("row", None)),
        out_specs=P("row", None),
        check_vma=False,
    )
```

time: 950 us -> 190 us (0.20)
  waiting for transfers between devices: 890 us -> 0 us
  Pallas kernels: 0 us -> 185 us
  matrix products: 18 us -> 0 us
  other arithmetic: 15.7 us -> 0 us
  between operations: 13.6 us -> 0.01 us
    psum x8 -> x0, waiting for transfers between devices: 889 us -> none  [the longest x4 302 us: broadcast(): return lax.psum(jnp.where(mine, value, jnp.zeros_like(value)), axis)]
    pallas_call x0 -> x1, Pallas kernels: none -> 185 us  [shards(): pl.pallas_call(kernel, out_shape=jax.ShapeDtypeStruct(rhs.shape, f32), in...]
    dot_general x4 -> x0, matrix products: 18 us -> none  [matmul(): jnp.dot(left, right, precision=lax.Precision.HIGHEST, preferred_element_t...]
  transfers between devices with their start and end apart: 8 -> 0, of which waited for: 8 -> 0; matrix products, arithmetic and copies ran while one was open for 0% -> 0% of each run, Pallas kernels for 0% -> 0%
where the time goes in v1:
time: 190 us
  Pallas kernels  185 us (97%)
  local copies, waits for them, and re-layouts  5.7 us (3%)
    pallas_call x1, Pallas kernels, shards(): pl.pallas_call(kernel, out_shape=jax.ShapeDtypeStruct(rhs.shape, f32), in...  185 us
    unnamed x1, local copies, waits for them, and re-layouts  5.7 us

profile of v1, /device:TPU:1, one launch (start us, length us, event | category | flops | bytes accessed | tf_op | source)
XLA Modules:
  0.0 190.3 jit_solution(9680863497760619500)
XLA Ops:
  0.0 184.6 %panel_steps.1 = f32[1280,1024]{1,0:T(8,128)} custom-call(f32[1280,512]{1,0:T(8,128)} %fac.1, f32[2,512,256]{2,1,0:T(8,128)} %inv.1, f32[1280,1024]{1,0:T(8,128)} %rhs.1), custom_call_target="tpu_custom_call" | custom-call | tf_op jit(solution)/shard_map/panel_steps/pallas_call | solution.py:440
  184.6 5.7 %copy.5 = f32[1280,1024]{1,0:T(8,128)} copy(f32[1280,1024]{1,0:T(8,128)} %panel_steps.1) | data formatting | bytes 10485760

commit v2 on v0

v2 whole, which is shorter than its diff:
```python
import functools

import jax
import jax.numpy as jnp
from jax import lax
from jax.experimental import pallas as pl
from jax.experimental.pallas import tpu as pltpu
from jax.sharding import PartitionSpec as P

MESH = pl.DeviceIdType.MESH
T = 256
W = 128
NY = 4
NQ = 8
NCH = 8
E = 32
WINDOW = 2


def kernel(fac, inv, rhs, out,
           G, PT, RB, XB, XS, B0, PA, RA, AB, RH, OA,
           lsem, bss, brs, gss, grs, dss, drs, rss, rrs, ass, ars,
           zss, zrs, oss, ors, ess, ers, fss, frs, yss):
    row = lax.axis_index("row")
    col = lax.axis_index("col")
    y, zl = lax.div(row, 2), lax.rem(row, 2)
    Q, c = lax.div(col, 2), lax.rem(col, 2)
    yo, so = lax.rem(Q, NY), lax.div(Q, NY)

    def dev(y_, zl_, q_, c_):
        return (2 * y_ + zl_, 2 * q_ + c_)

    def yy(d):
        return lax.rem(y + d, NY)

    def qq(d):
        return lax.rem(Q + d, NQ)

    up, down, far = yy(1), yy(3), yy(2)
    home = y == yo
    sib = dev(y, zl, Q, 1 - c)

    def remote(src, dst, ssem, rsem, device):
        return pltpu.make_async_remote_copy(
            src_ref=src, dst_ref=dst, send_sem=ssem, recv_sem=rsem,
            device_id=device, device_id_type=MESH)

    def arrived(r, sem):
        pltpu.make_async_copy(r, r, sem).wait()

    def signal(device):
        pl.semaphore_signal(bar, inc=1, device_id=device, device_id_type=MESH)

    bar = pltpu.get_barrier_semaphore()
    for e in range(1, NY * NQ):
        signal(dev(yy(e // NQ), zl, qq(e % NQ), c))
    signal(sib)
    signal(dev(y, 1 - zl, Q, c))
    pl.semaphore_wait(bar, NY * NQ + 1)

    def own(i):
        if i < 2:
            return inv.at[1, :, i]
        if i < 4:
            return fac.at[pl.ds(1, 2), i - 2, :, pl.ds(T, T)]
        if i < 6:
            return inv.at[0, :, i - 4]
        if i == 6:
            return fac.at[0, :, :, pl.ds(T, T)]
        return fac.at[0, :, :, pl.ds(0, T)]

    def blk(i, yb):
        return G.at[i, c, yb]

    def own_up(i):
        return remote(own(i), blk(i, y), gss.at[i, 0], grs.at[i, 0], dev(up, zl, Q, c))

    def own_down(i):
        return remote(own(i), blk(i, y), gss.at[i, 1], grs.at[i, 1], dev(down, zl, Q, c))

    def relay_up(i):
        r = G.at[i, c, down, 0]
        return remote(r, r, gss.at[i, 2], grs.at[i, 2], dev(up, zl, Q, c))

    def relay_down(i):
        r = G.at[i, c, up, 1]
        return remote(r, r, gss.at[i, 3], grs.at[i, 3], dev(down, zl, Q, c))

    def share(i, j):
        yb = (y, down, up, far)[j]
        src = own(i) if j == 0 else blk(i, yb)
        return remote(src, blk(i, yb), dss.at[i, j], drs.at[i, j], sib)

    def wait_share(i, j):
        yb = (y, down, up, far)[j]
        arrived(G.at[i, 1 - c, yb], drs.at[i, j])

    def send_own(i):
        own_up(i).start()
        own_down(i).start()

    def near(i):
        arrived(blk(i, down), grs.at[i, 0])
        relay_up(i).start()
        arrived(blk(i, up), grs.at[i, 1])
        relay_down(i).start()
        share(i, 1).start()
        share(i, 2).start()
        if i + WINDOW < NCH:
            send_own(i + WINDOW)

    def distant(i):
        arrived(G.at[i, c, far, 0], grs.at[i, 2])
        arrived(G.at[i, c, far, 1], grs.at[i, 3])
        share(i, 3).start()

    def cols(y_, c_):
        return pl.ds(pl.multiple_of((c_ * NY + y_) * W, W), W)

    def halfcols(c_):
        return pl.ds(pl.multiple_of(c_ * NY * W, NY * W), NY * W)

    def piece(q_):
        return pl.ds(pl.multiple_of(q_ * E, E), E)

    def b_dst(n, q_):
        return XB.at[0, zl, piece(q_)] if n == 0 else B0.at[piece(q_)]

    def b_each(n, do):
        for s in range(2):
            b = (3 if n == 0 else 1) + s
            qd = y + NY * s
            for d in range(NY):
                yd = yy(d)
                src = rhs.at[b, piece(Q), cols(yd, c)]
                dst = b_dst(n, Q)

                def far_copy():
                    return remote(src, dst, bss.at[n, s, d], brs.at[n, Q], dev(yd, zl, qd, c))
                if d == 0:
                    if do == "start":
                        @pl.when(qd == Q)
                        def _():
                            pltpu.make_async_copy(src, dst, brs.at[n, Q]).start()

                    @pl.when(qd != Q)
                    def _():
                        far_copy().start() if do == "start" else far_copy().wait_send()
                else:
                    far_copy().start() if do == "start" else far_copy().wait_send()

    def b_wait(n):
        for q_ in range(NQ):
            arrived(b_dst(n, q_), brs.at[n, q_])

    def halfrows(h):
        return pl.ds(h * (T // 2), T // 2)

    def zmove(st, h):
        r = XB.at[st, zl, halfrows(h)]
        return remote(r, r, zss.at[st, h], zrs.at[st, h], dev(y, 1 - zl, Q, c))

    def split(st, k, h):
        v = XB[st, k, halfrows(h), :]
        hi = v.astype(jnp.bfloat16)
        lo = (v - hi.astype(jnp.float32)).astype(jnp.bfloat16)
        XS[st, k, halfrows(h), pl.ds(0, W)] = hi
        XS[st, k, halfrows(h), pl.ds(W, W)] = lo

    def zdone(st):
        for h in range(2):
            arrived(XB.at[st, 1 - zl, halfrows(h)], zrs.at[st, h])
            split(st, 1 - zl, h)

    def product(i, yb, st):
        total = None
        for k in range(2):
            a = G[i, k, yb].reshape(T, T)
            hi = a.astype(jnp.bfloat16)
            lo = (a - hi.astype(jnp.float32)).astype(jnp.bfloat16)
            x = XS[st, k]
            wide = jnp.dot(hi, x, preferred_element_type=jnp.float32)
            part = wide[:, :W] + wide[:, W:] + jnp.dot(
                lo, x[:, :W], preferred_element_type=jnp.float32)
            total = part if total is None else total + part
        return total

    def scatter(ph, t, h):
        return remote(PT.at[ph, t, h], RB.at[ph, Q, h], rss.at[ph, t, h], rrs.at[ph, Q, h],
                      dev(y, zl, t, c))

    def tiles(i, ph, st, lo, hi):
        h = i % 2

        def step(j, carry):
            yb = lax.rem(y + 3 + j, NY)
            total = product(i, yb, st)
            for s in range(2):
                t = NY * s + yb
                PT[ph, t, h] = total[s * (T // 2):(s + 1) * (T // 2)]

                @pl.when(t != Q)
                def _():
                    scatter(ph, t, h).start()
            return carry

        lax.fori_loop(lo, hi, step, 0)

    def gathered(ph, h):
        def step(d, total):
            src = qq(d)
            arrived(RB.at[ph, src, h], rrs.at[ph, src, h])
            return total + RB[ph, src, h]
        return lax.fori_loop(1, NQ, step, PT[ph, Q, h])

    def o_each(n, do):
        st = 1 if n == 1 else 3
        for d in range(NQ):
            qd = qq(d)
            src = XB.at[st, zl, piece(qd)]
            dst = out.at[1 + 2 * n + so, piece(qd), cols(y, c)]
            sem = ors.at[n, NY * so + y]

            def far_copy():
                return remote(src, dst, oss.at[n, d], sem, dev(yo, zl, qd, c))
            if d == 0:
                if do == "start":
                    @pl.when(home)
                    def _():
                        pltpu.make_async_copy(src, dst, sem).start()

                @pl.when(jnp.logical_not(home))
                def _():
                    far_copy().start() if do == "start" else far_copy().wait_send()
            else:
                far_copy().start() if do == "start" else far_copy().wait_send()

    def o_spread(n, s, d):
        r = out.at[1 + 2 * n + s, piece(Q), halfcols(c)]
        return remote(r, r, ess.at[n, s, d], ers.at[n, s, Q], dev(y, zl, qq(d), c))

    def o_turn(n, s):
        for yb in range(NY):
            arrived(out.at[1 + 2 * n + s, piece(Q), cols(yb, c)], ors.at[n, NY * s + yb])
        for d in range(1, NQ):
            o_spread(n, s, d).start()

    def o_share(n):
        r = out.at[pl.ds(1 + 2 * n, 2), :, halfcols(c)]
        return remote(r, r, fss.at[n], frs.at[n], sib)

    def o_forward(n):
        for d in range(1, NQ):
            for s in range(2):
                arrived(out.at[1 + 2 * n + s, piece(qq(d)), halfcols(c)], ers.at[n, s, qq(d)])
        o_share(n).start()

    send_own(0)
    b_each(0, "start")
    share(0, 0).start()
    locals_ = [pltpu.make_async_copy(own(i), blk(i, y), lsem.at[i]) for i in range(NCH)]
    rh_copy = pltpu.make_async_copy(rhs.at[0], RH, lsem.at[NCH])
    for cp in locals_:
        cp.start()
    rh_copy.start()
    own_up(0).wait_send()
    own_down(0).wait_send()
    send_own(1)
    share(1, 0).start()
    b_wait(0)
    for h in range(2):
        zmove(0, h).start()
        split(0, zl, h)
    near(0)
    for cp in locals_:
        cp.wait()
    rh_copy.wait()
    for i in range(2, NCH):
        share(i, 0).start()
    zdone(0)
    for j in range(3):
        wait_share(0, j)
    tiles(0, 0, 0, 0, 3)
    near(1)
    distant(0)
    wait_share(0, 3)
    tiles(0, 0, 0, 3, 4)
    for j in range(3):
        wait_share(1, j)
    tiles(1, 0, 0, 0, 3)
    distant(1)
    wait_share(1, 3)
    tiles(1, 0, 0, 3, 4)
    b_each(1, "start")

    def sent(ph):
        def step(d, carry):
            scatter(ph, qq(d), 0).wait_send()
            scatter(ph, qq(d), 1).wait_send()
            return carry
        lax.fori_loop(1, NQ, step, 0)

    def finish(ph, st, h):
        total = gathered(ph, h)
        if st == 2:
            XB[st, zl, halfrows(h), :] = B0[halfrows(h), :] - total
        else:
            XB[st, zl, halfrows(h), :] = total
        zmove(st, h).start()
        split(st, zl, h)

    def whole(i, ph, st):
        for j in range(4):
            wait_share(i, j)
        tiles(i, ph, st, 0, 4)

    near(2)
    finish(0, 1, 0)
    finish(0, 1, 1)
    o_each(1, "start")
    distant(2)
    zdone(1)
    whole(2, 1, 1)
    near(3)
    distant(3)
    whole(3, 1, 1)
    near(4)
    b_wait(1)
    sent(1)
    o_turn(1, 0)
    finish(1, 2, 0)
    distant(4)
    near(5)
    finish(1, 2, 1)
    o_turn(1, 1)
    zdone(2)
    whole(4, 2, 2)
    distant(5)
    whole(5, 2, 2)
    near(6)
    distant(6)
    near(7)
    o_forward(1)
    for j in range(4):
        wait_share(6, j)

    def above_one(j, carry):
        yb = lax.rem(y + 3 + j, NY)
        PA[yb] = product(6, yb, 1)
        return carry
    lax.fori_loop(0, NY, above_one, 0)
    finish(2, 3, 0)
    finish(2, 3, 1)
    o_each(0, "start")
    distant(7)
    zdone(3)
    for j in range(4):
        wait_share(7, j)

    def above_two(j, carry):
        yb = lax.rem(y + 3 + j, NY)
        PA[yb] = PA[yb] + product(7, yb, 3)
        return carry
    lax.fori_loop(0, NY, above_two, 0)

    def a_each(do):
        for e in range(NY * NQ):
            yd, qd = yy(e // NQ), qq(e % NQ)
            src, dst = PA.at[yd, piece(qd)], RA.at[y, Q]
            if e == 0:
                if do == "start":
                    pltpu.make_async_copy(src, dst, ars.at[y]).start()
            else:
                far_copy = remote(src, dst, ass.at[e], ars.at[y], dev(yd, zl, qd, c))
                far_copy.start() if do == "start" else far_copy.wait_send()

    a_each("start")
    a_each("end")
    o_turn(0, 0)
    for yb in range(NY):
        arrived(RA.at[yb], ars.at[yb])
        total = RA[yb, 0]
        for q_ in range(1, NQ):
            total = total + RA[yb, q_]
        AB[piece(Q), cols(yb, c)] = total

    def a_part(q_, c_):
        return AB.at[piece(q_), halfcols(c_)]

    def a_spread(d):
        return remote(a_part(Q, c), a_part(Q, c), ess.at[2, 0, d], ers.at[2, 0, Q],
                      dev(y, zl, qq(d), c))

    def a_share(d):
        r = a_part(qq(d), c)
        return remote(r, r, yss.at[d], frs.at[2 + qq(d)], sib)

    for d in range(1, NQ):
        a_spread(d).start()
    a_share(0).start()
    o_turn(0, 1)
    for d in range(1, NQ):
        arrived(a_part(qq(d), c), ers.at[2, 0, qq(d)])
        a_share(d).start()
    OA[:, halfcols(c)] = RH[:, halfcols(c)] - AB[:, halfcols(c)]
    w0 = pltpu.make_async_copy(OA.at[:, halfcols(c)], out.at[0, :, halfcols(c)], lsem.at[0])
    w0.start()
    for d in range(NQ):
        arrived(a_part(qq(d), 1 - c), frs.at[2 + qq(d)])
    OA[:, halfcols(1 - c)] = RH[:, halfcols(1 - c)] - AB[:, halfcols(1 - c)]
    w1 = pltpu.make_async_copy(OA.at[:, halfcols(1 - c)], out.at[0, :, halfcols(1 - c)], lsem.at[1])
    w1.start()
    o_forward(0)

    for n in range(2):
        arrived(out.at[pl.ds(1 + 2 * n, 2), :, halfcols(1 - c)], frs.at[n])
    w0.wait()
    w1.wait()
    for i in range(NCH):
        if i:
            own_up(i).wait_send()
            own_down(i).wait_send()
        relay_up(i).wait_send()
        relay_down(i).wait_send()
        for j in range(4):
            share(i, j).wait_send()
    sent(0)
    sent(2)
    for st in range(4):
        zmove(st, 0).wait_send()
        zmove(st, 1).wait_send()
    for n in range(2):
        b_each(n, "end")
        o_each(n, "end")
        for d in range(1, NQ):
            o_spread(n, 0, d).wait_send()
            o_spread(n, 1, d).wait_send()
        o_share(n).wait_send()
    for d in range(1, NQ):
        a_spread(d).wait_send()
    for d in range(NQ):
        a_share(d).wait_send()


def shards(factor, inverse, rhs):
    f32, bf16 = jnp.float32, jnp.bfloat16
    dma = pltpu.SemaphoreType.DMA
    solved = pl.pallas_call(
        kernel,
        out_shape=jax.ShapeDtypeStruct((5, T, NQ * W), f32),
        in_specs=[pl.BlockSpec(memory_space=pl.ANY)] * 3,
        out_specs=pl.BlockSpec(memory_space=pl.ANY),
        scratch_shapes=[
            pltpu.VMEM((NCH, 2, NY, 2, T // 2, T), f32),
            pltpu.VMEM((3, NQ, 2, T // 2, W), f32),
            pltpu.VMEM((3, NQ, 2, T // 2, W), f32),
            pltpu.VMEM((4, 2, T, W), f32),
            pltpu.VMEM((4, 2, T, 2 * W), bf16),
            pltpu.VMEM((T, W), f32),
            pltpu.VMEM((NY, T, W), f32),
            pltpu.VMEM((NY, NQ, E, W), f32),
            pltpu.VMEM((T, NQ * W), f32),
            pltpu.VMEM((T, NQ * W), f32),
            pltpu.VMEM((T, NQ * W), f32),
            dma((NCH + 1,)),
            dma((2, 2, NY)), dma((2, NQ)),
            dma((NCH, 4)), dma((NCH, 4)),
            dma((NCH, 4)), dma((NCH, 4)),
            dma((3, NQ, 2)), dma((3, NQ, 2)),
            dma((NY * NQ,)), dma((NY,)),
            dma((4, 2)), dma((4, 2)),
            dma((2, NQ)), dma((2, NQ)),
            dma((3, 2, NQ)), dma((3, 2, NQ)),
            dma((2,)), dma((2 + NQ,)),
            dma((NQ,)),
        ],
        compiler_params=pltpu.CompilerParams(
            collective_id=0, has_side_effects=True, vmem_limit_bytes=56 * 2**20),
        name="panel_steps",
    )(factor.reshape(5, 2, T // 2, 2 * T), inverse.reshape(2, 2, 2, T // 2, T),
      rhs.reshape(5, T, NQ * W))
    return solved.reshape(rhs.shape)


def solution(mesh):
    return jax.shard_map(
        shards,
        mesh=mesh,
        in_specs=(P("row", "col"), P(None, "row", "col"), P("row", None)),
        out_specs=P("row", None),
        check_vma=False,
    )
```

time: 950 us -> 145 us (0.15)
  waiting for transfers between devices: 890 us -> 0 us
  Pallas kernels: 0 us -> 139 us
  matrix products: 18 us -> 0 us
  other arithmetic: 15.7 us -> 0 us
  between operations: 13.6 us -> 0.01 us
    psum x8 -> x0, waiting for transfers between devices: 889 us -> none  [the longest x4 302 us: broadcast(): return lax.psum(jnp.where(mine, value, jnp.zeros_like(value)), axis)]
    pallas_call x0 -> x1, Pallas kernels: none -> 139 us  [shards(): pl.pallas_call(kernel, out_shape=jax.ShapeDtypeStruct((5, T, NQ * W), f32...]
    dot_general x4 -> x0, matrix products: 18 us -> none  [matmul(): jnp.dot(left, right, precision=lax.Precision.HIGHEST, preferred_element_t...]
  transfers between devices with their start and end apart: 8 -> 0, of which waited for: 8 -> 0; matrix products, arithmetic and copies ran while one was open for 0% -> 0% of each run, Pallas kernels for 0% -> 0%
where the time goes in v2:
time: 145 us
  Pallas kernels  139 us (96%)
  local copies, waits for them, and re-layouts  5.7 us (4%)
    pallas_call x1, Pallas kernels, shards(): pl.pallas_call(kernel, out_shape=jax.ShapeDtypeStruct((5, T, NQ * W), f32...  139 us
    unnamed x1, local copies, waits for them, and re-layouts  5.7 us

profile of v2, /device:TPU:1, one launch (start us, length us, event | category | flops | bytes accessed | tf_op | source)
XLA Modules:
  0.0 144.6 jit_solution(13826516628208489804)
XLA Ops:
  0.0 138.9 %panel_steps.1 = f32[5,256,1024]{2,1,0:T(8,128)} custom-call(f32[5,2,128,512]{3,2,1,0:T(8,128)} %bitcast.6, f32[2,2,2,128,256]{4,3,2,1,0:T(8,128)} %bitcast.7, f32[5,256,1024]{2,1,0:T(8,128)} %bitcast.5), custom_call_target="tpu_custom_call" | custom-call | tf_op jit(solution)/shard_map/panel_steps/pallas_call | solution.py:448
  138.9 5.7 %copy.5 = f32[1280,1024]{1,0:T(8,128)} copy(f32[1280,1024]{1,0:T(8,128)} %bitcast.4) | data formatting | bytes 10485760

commit v3 on v2

--- a/solution.py
+++ b/solution.py
@@ -18,9 +18,9 @@
 
 
 def kernel(fac, inv, rhs, out,
-           G, PT, RB, XB, XS, B0, PA, RA, AB, RH, OA,
+           G, PT, RB, XB, XS, B0, PA, RA, AB, RH,
            lsem, bss, brs, gss, grs, dss, drs, rss, rrs, ass, ars,
-           zss, zrs, oss, ors, ess, ers, fss, frs, yss):
+           zss, zrs, oss, ors, ess, ers, fss, frs, yss, ars2):
     row = lax.axis_index("row")
     col = lax.axis_index("col")
     y, zl = lax.div(row, 2), lax.rem(row, 2)
@@ -245,15 +245,14 @@
         for d in range(1, NQ):
             o_spread(n, s, d).start()
 
-    def o_share(n):
-        r = out.at[pl.ds(1 + 2 * n, 2), :, halfcols(c)]
-        return remote(r, r, fss.at[n], frs.at[n], sib)
-
-    def o_forward(n):
+    def o_share(n, s):
+        r = out.at[1 + 2 * n + s, :, halfcols(c)]
+        return remote(r, r, fss.at[n, s], frs.at[n, s], sib)
+
+    def o_forward(n, s):
         for d in range(1, NQ):
-            for s in range(2):
-                arrived(out.at[1 + 2 * n + s, piece(qq(d)), halfcols(c)], ers.at[n, s, qq(d)])
-        o_share(n).start()
+            arrived(out.at[1 + 2 * n + s, piece(qq(d)), halfcols(c)], ers.at[n, s, qq(d)])
+        o_share(n, s).start()
 
     send_own(0)
     b_each(0, "start")
@@ -340,7 +339,8 @@
     near(6)
     distant(6)
     near(7)
-    o_forward(1)
+    o_forward(1, 0)
+    o_forward(1, 1)
     for j in range(4):
         wait_share(6, j)
 
@@ -393,29 +393,25 @@
 
     def a_share(d):
         r = a_part(qq(d), c)
-        return remote(r, r, yss.at[d], frs.at[2 + qq(d)], sib)
+        return remote(r, r, yss.at[d], ars2.at[qq(d)], sib)
 
     for d in range(1, NQ):
         a_spread(d).start()
     a_share(0).start()
     o_turn(0, 1)
+    o_forward(0, 0)
     for d in range(1, NQ):
         arrived(a_part(qq(d), c), ers.at[2, 0, qq(d)])
         a_share(d).start()
-    OA[:, halfcols(c)] = RH[:, halfcols(c)] - AB[:, halfcols(c)]
-    w0 = pltpu.make_async_copy(OA.at[:, halfcols(c)], out.at[0, :, halfcols(c)], lsem.at[0])
-    w0.start()
+    out[0, :, halfcols(c)] = RH[:, halfcols(c)] - AB[:, halfcols(c)]
+    o_forward(0, 1)
     for d in range(NQ):
-        arrived(a_part(qq(d), 1 - c), frs.at[2 + qq(d)])
-    OA[:, halfcols(1 - c)] = RH[:, halfcols(1 - c)] - AB[:, halfcols(1 - c)]
-    w1 = pltpu.make_async_copy(OA.at[:, halfcols(1 - c)], out.at[0, :, halfcols(1 - c)], lsem.at[1])
-    w1.start()
-    o_forward(0)
+        arrived(a_part(qq(d), 1 - c), ars2.at[qq(d)])
+    out[0, :, halfcols(1 - c)] = RH[:, halfcols(1 - c)] - AB[:, halfcols(1 - c)]
 
     for n in range(2):
-        arrived(out.at[pl.ds(1 + 2 * n, 2), :, halfcols(1 - c)], frs.at[n])
-    w0.wait()
-    w1.wait()
+        for s in range(2):
+            arrived(out.at[1 + 2 * n + s, :, halfcols(1 - c)], frs.at[n, s])
     for i in range(NCH):
         if i:
             own_up(i).wait_send()
@@ -435,7 +431,8 @@
         for d in range(1, NQ):
             o_spread(n, 0, d).wait_send()
             o_spread(n, 1, d).wait_send()
-        o_share(n).wait_send()
+        for s in range(2):
+            o_share(n, s).wait_send()
     for d in range(1, NQ):
         a_spread(d).wait_send()
     for d in range(NQ):
@@ -447,9 +444,9 @@
     dma = pltpu.SemaphoreType.DMA
     solved = pl.pallas_call(
         kernel,
-        out_shape=jax.ShapeDtypeStruct((5, T, NQ * W), f32),
-        in_specs=[pl.BlockSpec(memory_space=pl.ANY)] * 3,
-        out_specs=pl.BlockSpec(memory_space=pl.ANY),
+        out_shape=pltpu.VMEM((5, T, NQ * W), f32),
+        in_specs=[pl.BlockSpec(memory_space=pltpu.HBM)] * 3,
+        out_specs=pl.BlockSpec(memory_space=pltpu.VMEM),
         scratch_shapes=[
             pltpu.VMEM((NCH, 2, NY, 2, T // 2, T), f32),
             pltpu.VMEM((3, NQ, 2, T // 2, W), f32),
@@ -461,7 +458,6 @@
             pltpu.VMEM((NY, NQ, E, W), f32),
             pltpu.VMEM((T, NQ * W), f32),
             pltpu.VMEM((T, NQ * W), f32),
-            pltpu.VMEM((T, NQ * W), f32),
             dma((NCH + 1,)),
             dma((2, 2, NY)), dma((2, NQ)),
             dma((NCH, 4)), dma((NCH, 4)),
@@ -471,8 +467,8 @@
             dma((4, 2)), dma((4, 2)),
             dma((2, NQ)), dma((2, NQ)),
             dma((3, 2, NQ)), dma((3, 2, NQ)),
-            dma((2,)), dma((2 + NQ,)),
-            dma((NQ,)),
+            dma((2, 2)), dma((2, 2)),
+            dma((NQ,)), dma((NQ,)),
         ],
         compiler_params=pltpu.CompilerParams(
             collective_id=0, has_side_effects=True, vmem_limit_bytes=56 * 2**20),

time: 145 us -> 138 us (0.952)
  local copies, waits for them, and re-layouts: 5.7 us -> 2.36 us
  Pallas kernels: 139 us -> 136 us
    unnamed x1, local copies, waits for them, and re-layouts: 5.7 us -> 2.36 us
    pallas_call x1, Pallas kernels: 139 us -> 136 us  [shards(): pl.pallas_call(kernel, out_shape=pltpu.VMEM((5, T, NQ * W), f32), in_spec...]
where the time goes in v3:
time: 138 us
  Pallas kernels  136 us (99%)
  local copies, waits for them, and re-layouts  2.36 us (2%)
    pallas_call x1, Pallas kernels, shards(): pl.pallas_call(kernel, out_shape=pltpu.VMEM((5, T, NQ * W), f32), in_spec...  136 us

profile of v3, /device:TPU:1, one launch (start us, length us, event | category | flops | bytes accessed | tf_op | source)
XLA Modules:
  0.0 138.2 jit_solution(3553389115223704002)
XLA Ops:
  0.0 135.8 %panel_steps.1 = f32[5,256,1024]{2,1,0:T(8,128)S(1)} custom-call(f32[5,2,128,512]{3,2,1,0:T(8,128)} %bitcast.6, f32[2,2,2,128,256]{4,3,2,1,0:T(8,128)} %bitcast.7, f32[5,256,1024]{2,1,0:T(8,128)} %bitcast.5), custom_call_target="tpu_custom_call" | custom-call | tf_op jit(solution)/shard_map/panel_steps/pallas_call | solution.py:445
  135.8 2.4 %copy.5 = f32[1280,1024]{1,0:T(8,128)} copy(f32[1280,1024]{1,0:T(8,128)S(1)} %bitcast.4) | data formatting | bytes 10485760

commit v4 on v3

--- a/solution.py
+++ b/solution.py
@@ -325,10 +325,10 @@
     whole(3, 1, 1)
     near(4)
     b_wait(1)
+    distant(4)
     sent(1)
     o_turn(1, 0)
     finish(1, 2, 0)
-    distant(4)
     near(5)
     finish(1, 2, 1)
     o_turn(1, 1)

time: 138 us -> 136 us (0.986)
  Pallas kernels: 136 us -> 133 us
    pallas_call x1, Pallas kernels: 136 us -> 133 us  [shards(): pl.pallas_call(kernel, out_shape=pltpu.VMEM((5, T, NQ * W), f32), in_spec...]
where the time goes in v4:
time: 136 us
  Pallas kernels  133 us (98%)
  local copies, waits for them, and re-layouts  2.36 us (2%)
    pallas_call x1, Pallas kernels, shards(): pl.pallas_call(kernel, out_shape=pltpu.VMEM((5, T, NQ * W), f32), in_spec...  133 us

profile of v4, /device:TPU:1, one launch (start us, length us, event | category | flops | bytes accessed | tf_op | source)
XLA Modules:
  0.0 135.8 jit_solution(9505260812053993717)
XLA Ops:
  0.0 133.5 %panel_steps.1 = f32[5,256,1024]{2,1,0:T(8,128)S(1)} custom-call(f32[5,2,128,512]{3,2,1,0:T(8,128)} %bitcast.6, f32[2,2,2,128,256]{4,3,2,1,0:T(8,128)} %bitcast.7, f32[5,256,1024]{2,1,0:T(8,128)} %bitcast.5), custom_call_target="tpu_custom_call" | custom-call | tf_op jit(solution)/shard_map/panel_steps/pallas_call | solution.py:445
  133.5 2.4 %copy.5 = f32[1280,1024]{1,0:T(8,128)} copy(f32[1280,1024]{1,0:T(8,128)S(1)} %bitcast.4) | data formatting | bytes 10485760

commit v5 on v4

--- a/solution.py
+++ b/solution.py
@@ -375,7 +375,6 @@
                 far_copy.start() if do == "start" else far_copy.wait_send()
 
     a_each("start")
-    a_each("end")
     o_turn(0, 0)
     for yb in range(NY):
         arrived(RA.at[yb], ars.at[yb])
@@ -409,6 +408,7 @@
         arrived(a_part(qq(d), 1 - c), ars2.at[qq(d)])
     out[0, :, halfcols(1 - c)] = RH[:, halfcols(1 - c)] - AB[:, halfcols(1 - c)]
 
+    a_each("end")
     for n in range(2):
         for s in range(2):
             arrived(out.at[1 + 2 * n + s, :, halfcols(1 - c)], frs.at[n, s])

time: 136 us -> 136 us (level)
  no operation moved by 1% of the time
where the time goes in v5:
time: 136 us
  Pallas kernels  133 us (98%)
  local copies, waits for them, and re-layouts  2.36 us (2%)
    pallas_call x1, Pallas kernels, shards(): pl.pallas_call(kernel, out_shape=pltpu.VMEM((5, T, NQ * W), f32), in_spec...  133 us

profile of v5, /device:TPU:1, one launch (start us, length us, event | category | flops | bytes accessed | tf_op | source)
XLA Modules:
  0.0 135.6 jit_solution(14627410885323342258)
XLA Ops:
  0.0 133.3 %panel_steps.1 = f32[5,256,1024]{2,1,0:T(8,128)S(1)} custom-call(f32[5,2,128,512]{3,2,1,0:T(8,128)} %bitcast.6, f32[2,2,2,128,256]{4,3,2,1,0:T(8,128)} %bitcast.7, f32[5,256,1024]{2,1,0:T(8,128)} %bitcast.5), custom_call_target="tpu_custom_call" | custom-call | tf_op jit(solution)/shard_map/panel_steps/pallas_call | solution.py:445
  133.3 2.4 %copy.5 = f32[1280,1024]{1,0:T(8,128)} copy(f32[1280,1024]{1,0:T(8,128)S(1)} %bitcast.4) | data formatting | bytes 10485760

commit v6 on v5

--- a/solution.py
+++ b/solution.py
@@ -207,11 +207,12 @@
         lax.fori_loop(lo, hi, step, 0)
 
     def gathered(ph, h):
-        def step(d, total):
+        total = PT[ph, Q, h]
+        for d in range(1, NQ):
             src = qq(d)
             arrived(RB.at[ph, src, h], rrs.at[ph, src, h])
-            return total + RB[ph, src, h]
-        return lax.fori_loop(1, NQ, step, PT[ph, Q, h])
+            total = total + RB[ph, src, h]
+        return total
 
     def o_each(n, do):
         st = 1 if n == 1 else 3

time: 136 us -> 136 us (level)
  no operation moved by 1% of the time
where the time goes in v6:
time: 136 us
  Pallas kernels  133 us (98%)
  local copies, waits for them, and re-layouts  2.36 us (2%)
    pallas_call x1, Pallas kernels, shards(): pl.pallas_call(kernel, out_shape=pltpu.VMEM((5, T, NQ * W), f32), in_spec...  133 us

profile of v6, /device:TPU:1, one launch (start us, length us, event | category | flops | bytes accessed | tf_op | source)
XLA Modules:
  0.0 135.6 jit_solution(5212669564002970528)
XLA Ops:
  0.0 133.2 %panel_steps.1 = f32[5,256,1024]{2,1,0:T(8,128)S(1)} custom-call(f32[5,2,128,512]{3,2,1,0:T(8,128)} %bitcast.6, f32[2,2,2,128,256]{4,3,2,1,0:T(8,128)} %bitcast.7, f32[5,256,1024]{2,1,0:T(8,128)} %bitcast.5), custom_call_target="tpu_custom_call" | custom-call | tf_op jit(solution)/shard_map/panel_steps/pallas_call | solution.py:446
  133.2 2.4 %copy.5 = f32[1280,1024]{1,0:T(8,128)} copy(f32[1280,1024]{1,0:T(8,128)S(1)} %bitcast.4) | data formatting | bytes 10485760
